TPU v7x, 32 devices: a whole 2x2x4 slice. The times are simulated.
32 devices in a mesh: grp: 4 (over y, core), shard: 8 (over z, x).
Axes of the slice: x: 2, y: 2, z: 4, core: 2. Of those that a mesh axis runs over, the one named last changes fastest.
Arguments:
- regressors: bfloat16 [98304, 512], P(('grp', 'shard')), may hold values from -40 to 40
- targets: bfloat16 [98304, 512], P(('grp', 'shard')), may hold values from -120 to 120
Outputs:
- predictor: float32 [512, 512], replicated
- residuals: bfloat16 [98304, 512], P(('grp', 'shard'))
All inputs are finite; a program needn't handle non-finite values.
Results may differ from a plain program's by a relative error of at most 0.0013.
Values sent between devices are 32-bit elements; how exact they have to be, the bound alone decides.
A program may use at most 64 MiB of HBM per device.

v0:
```python
import jax
import jax.numpy as jnp
from jax import lax
from jax.sharding import PartitionSpec as P


def solve_predictor(factor, cross_sum):
    interim = jax.scipy.linalg.solve_triangular(factor, cross_sum, lower=True)
    return jax.scipy.linalg.solve_triangular(factor, interim, lower=True, trans=1)


def residual_block(rows_x, rows_y, predictor):
    pred_high = predictor.astype(jnp.bfloat16)
    pred_low = (predictor - lax.optimization_barrier(pred_high).astype(jnp.float32)).astype(
        jnp.bfloat16
    )
    estimate = jnp.dot(rows_x, pred_high, preferred_element_type=jnp.float32) + jnp.dot(
        rows_x, pred_low, preferred_element_type=jnp.float32
    )
    return (rows_y.astype(jnp.float32) - estimate).astype(jnp.bfloat16)


def body(regressors, targets):
    contract = (((0,), (0,)), ((), ()))
    gram_local = lax.dot_general(
        regressors, regressors, contract, preferred_element_type=jnp.float32
    )
    cross_local = lax.dot_general(regressors, targets, contract, preferred_element_type=jnp.float32)
    gram_total, cross_total = lax.psum((gram_local, cross_local), ("grp", "shard"))
    predictor = solve_predictor(jnp.linalg.cholesky(gram_total), cross_total)
    residuals = residual_block(regressors, targets, predictor)
    return (predictor, residuals)


def solution(mesh):
    placed = (P(("grp", "shard"), None), P(("grp", "shard"), None))
    return jax.shard_map(
        body,
        mesh=mesh,
        in_specs=placed,
        out_specs=(P(), P(("grp", "shard"), None)),
        check_vma=False,
    )
```

profile of v0, /device:TPU:0, one launch (start us, length us, event | category | flops | bytes accessed | tf_op | source)
XLA Modules:
  0.0 333.7 jit_solution(5456614522378130014)
XLA Ops:
  7.2 1.8 copy-done
  9.1 2.8 fusion.50
  11.9 2.8 fusion.51
  14.7 4.8 %copy.6 = bf16[3072,512]{0,1:T(8,128)(2,1)} copy(bf16[3072,512]{1,0:T(8,128)(2,1)} %param.3) | data formatting | bytes 6291456 | tf_op args[1]
  19.5 132.2 %all-reduce.4.cloned.1.call-done = (f32[512,512]{1,0:T(8,128)}, f32[512,512]{0,1:T(8,128)}) async-done(((f32[512,512]{1,0:T(8,128)}, f32[512,512]{0,1:T(8,128)}), (f32[512,512]{1,0:T(8,128)}, f32[512,512]{0,1:T(8,128)})) %all-reduce.4.cloned.1.call-update) | async-done | bytes 2097168 | tf_op jit(solution)/shard_map/psum | solution.py:29
  151.7 2.5 copy.5
  154.3 1.8 fusion.1
  157.1 11.7 %cholesky.104 = f32[128,128]{1,0:T(8,128)S(1)} custom-call(f32[128,128]{1,0:T(8,128)S(1)} %cholesky.266), custom_call_target="Cholesky" | custom-call | tf_op jit(solution)/shard_map/jit(cholesky)/cholesky | solution.py:30
  168.8 9.8 %custom-call.34 = f32[1,128,128]{1,2,0:T(8,128)S(1)} custom-call(f32[1,128,128]{2,1,0:T(8,128)S(1)} %get-tuple-element.35), custom_call_target="InvertDiagBlocksLowerTriangular" | custom-call | tf_op jit(solution)/shard_map/jit(cholesky)/cholesky | solution.py:30
  179.7 1.9 constant_dynamic-update-slice_fusion.3
  181.7 1.2 convolution_subtract_fusion.6
  182.9 11.7 %cholesky.217 = f32[128,128]{1,0:T(8,128)S(1)} custom-call(f32[128,128]{1,0:T(8,128)S(1)} %cholesky.270), custom_call_target="Cholesky" | custom-call | tf_op jit(solution)/shard_map/jit(cholesky)/cholesky | solution.py:30
  195.3 10.0 %custom-call.35 = f32[1,128,128]{1,2,0:T(8,128)S(1)} custom-call(f32[1,128,128]{2,1,0:T(8,128)S(1)} %get-tuple-element.32), custom_call_target="InvertDiagBlocksLowerTriangular" | custom-call | tf_op jit(solution)/shard_map/jit(cholesky)/cholesky | solution.py:30
  206.2 1.4 convolution_subtract_fusion.7
  207.6 11.7 %cholesky.238 = f32[128,128]{1,0:T(8,128)S(1)} custom-call(f32[128,128]{1,0:T(8,128)S(1)} %cholesky.275), custom_call_target="Cholesky" | custom-call | tf_op jit(solution)/shard_map/jit(cholesky)/cholesky | solution.py:30
  220.6 9.8 %custom-call.36 = f32[1,128,128]{1,2,0:T(8,128)S(1)} custom-call(f32[1,128,128]{2,1,0:T(8,128)S(1)} %get-tuple-element.29), custom_call_target="InvertDiagBlocksLowerTriangular" | custom-call | tf_op jit(solution)/shard_map/jit(cholesky)/cholesky | solution.py:30
  231.3 1.4 convolution_subtract_fusion.8
  232.7 11.7 %cholesky.255 = f32[128,128]{1,0:T(8,128)S(1)} custom-call(f32[128,128]{1,0:T(8,128)S(1)} %convolution_subtract_fusion.8), custom_call_target="Cholesky" | custom-call | tf_op jit(solution)/shard_map/jit(cholesky)/cholesky | solution.py:30
  248.8 2.6 select_select_fusion
  251.3 14.1 %while.1 = (s32[]{:T(128)}, f32[512,512]{1,0:T(8,128)}, s32[4,2]{0,1:T(2,128)S(1)}, f32[4,128,128]{2,1,0:T(8,128)}, s32[]{:T(128)}) while((s32[]{:T(128)}, f32[512,512]{1,0:T(8,128)}, s32[4,2]{0,1:T(2,128)S(1)}, f32[4,128,128]{2,1,0:T(8,128)}, s32[]{:T(128)}) %tuple.33), condition=%wide.while_cond, body=%wide.while_body.sunk | while | flops 2 | bytes 132205 | solution.py:9
  252.0 2.9 bitcast_dynamic-update-slice_fusion.2
  255.5 2.9 bitcast_dynamic-update-slice_fusion.2
  259.1 2.9 bitcast_dynamic-update-slice_fusion.2
  262.6 2.8 bitcast_dynamic-update-slice_fusion.2
  265.4 40.1 %custom-call.37 = f32[4,128,128]{1,2,0:T(8,128)S(1)} custom-call(f32[4,128,128]{2,1,0:T(8,128)} %get-tuple-element.9), custom_call_target="InvertDiagBlocksLowerTriangular" | custom-call | tf_op jit(solution)/shard_map/jit(_solve_triangular)/triangular_solve | solution.py:9
  305.6 1.5 fusion.18
  307.0 1.4 convolution_subtract_fusion.3
  308.8 1.4 convolution_subtract_fusion.2
  310.7 1.6 convolution_subtract_fusion.5
  316.0 1.9 fusion.52
  318.3 3.5 %fusion = bf16[3072,512]{0,1:T(8,128)(2,1)} fusion(f32[512,3072]{1,0:T(8,128)S(1)} %fusion.52, bf16[3072,512]{0,1:T(8,128)(2,1)S(1)} %copy-done.1, bf16[3072,512]{1,0:T(8,128)(2,1)S(1)} %copy-done, f32[512,512]{1,0:T(8,128)S(1)} %get-tuple-element.23, bf16[512,512]{1,0:T(8,128)(2,1)S(1)} %get-tuple-element.22), kind=kOutput, calls=%fused_computation.3 | convolution fusion | flops 1617690624 | bytes 17301504 | tf_op jit(solution)/shard_map/dot_general | solution.py:17
  321.8 4.6 %copy.7 = bf16[3072,512]{1,0:T(8,128)(2,1)} copy(bf16[3072,512]{0,1:T(8,128)(2,1)} %fusion) | data formatting | bytes 6291456
  (48 shorter events, 15.4 us)
Async XLA Ops:
  7.2 1.9 copy-start
  7.2 144.6 %all-reduce.4.cloned.1.call-start = ((), (), s32[]{:S(2)}) async-start(), calls=%async_computation | async-start | bytes 4194304 | tf_op jit(solution)/shard_map/psum | solution.py:29
  9.1 2.8 copy-start.4
  156.0 1.0 copy-start.5
  305.6 5.2 %copy-start.2 = (f32[512,512]{1,0:T(8,128)S(1)}, f32[512,512]{1,0:T(8,128)}, u32[]{:S(2)}) copy-start(f32[512,512]{1,0:T(8,128)} %get-tuple-element.88) | copy-start | bytes 3145732
  316.0 1.9 copy-start.3
  316.0 2.3 copy-start.1
Sparse Core Ops, SparseCore 0:
  14.8 136.8 all-reduce.3
where the time goes:
time: 337 us; the launch traced here: 334 us
  waiting for transfers between devices  132 us (39%)
  other arithmetic  125 us (37%)
  local copies, waits for them, and re-layouts  30.5 us (9%)
  matrix products  28.9 us (9%)
  between operations  17.1 us (5%)
    psum x1, waiting for transfers between devices, body(): lax.psum((gram_local, cross_local), ('grp', 'shard'))  132 us
    another operation x14, other arithmetic, body(): predictor = solve_predictor(jnp.linalg.cholesky(gram_total), cross_total)  80.4 us
    another operation x3, other arithmetic, solve_predictor(): jax.scipy.linalg.solve_triangular(factor, interim, lower=True, trans=1)  42.7 us
    another operation x12, local copies, waits for them, and re-layouts  14.1 us
    unnamed x14, local copies, waits for them, and re-layouts  12.7 us
    another operation x6, matrix products, body(): predictor = solve_predictor(jnp.linalg.cholesky(gram_total), cross_total)  7.76 us
    another operation x7, matrix products, solve_predictor(): interim = jax.scipy.linalg.solve_triangular(factor, cross_sum, lower=True)  7.11 us
  transfers between devices with their start and end apart: 1, of which 1 were waited for; matrix products, arithmetic and copies ran while one was open for 1% of the time, Pallas kernels for 0%

commit v1 on v0

v1 whole, which is shorter than its diff:
```python
import functools

import jax
import jax.numpy as jnp
from jax import lax
from jax.experimental import pallas as pl
from jax.experimental.pallas import tpu as pltpu
from jax.sharding import PartitionSpec as P

MESH = pl.DeviceIdType.MESH
BLK = 128
GRP8 = 8
HIGHEST = lax.Precision.HIGHEST


def dot32(a, b):
    return jnp.dot(a, b, preferred_element_type=jnp.float32, precision=HIGHEST)


def phases(n_grp, n_shard):
    g, s = lax.axis_index("grp"), lax.axis_index("shard")
    cores = 2 if n_grp % 2 == 0 else 1
    ny = n_grp // cores
    nx = ny if n_shard % ny == 0 else 1
    nz = n_shard // nx
    y, core = g // cores, g % cores
    z, x = s // nx, s % nx
    core_ph = (cores, core, lambda q: (y * cores + q, s))
    plane_ph = (
        ny * nx,
        y * nx + x,
        lambda q: ((q // nx) * cores + core, z * nx + q % nx),
    )
    line_ph = (nz, z, lambda q: (g, q * nx + x))
    return core_ph, plane_ph, line_ph


def split_rows(rows, n):
    unit = 8 * n
    units = rows // unit
    first = max(1, (units * 2 + 1) // 3)
    if units < 2:
        return (rows,)
    return (first * unit, (units - first) * unit)


def part_phases(n_grp, n_shard, n_parts):
    a, b, c = phases(n_grp, n_shard)
    orders = [(a, b, c), (a, c, b)][:n_parts]
    return orders


def phase_sizes(n_grp, n_shard, n_parts):
    cores = 2 if n_grp % 2 == 0 else 1
    ny = n_grp // cores
    nx = ny if n_shard % ny == 0 else 1
    nz = n_shard // nx
    return [(cores, ny * nx, nz), (cores, nz, ny * nx)][:n_parts]


def reduce_kernel(n_grp, n_shard, parts, in_ref, out_ref, *scratch):
    n_parts = len(parts)
    recv = [scratch[3 * p : 3 * p + 3] for p in range(n_parts)]
    acc, send_sem, recv_sem, send2, recv2 = scratch[3 * n_parts :]
    orders = part_phases(n_grp, n_shard, n_parts)

    barrier = pltpu.get_barrier_semaphore()
    count = 0
    for m, me, dev in orders[0]:
        for d in range(1, m):
            pl.semaphore_signal(
                barrier, inc=1, device_id=dev((me + d) % m), device_id_type=MESH
            )
            count += 1
    pl.semaphore_wait(barrier, count)

    starts = [sum(parts[:p]) for p in range(n_parts)]
    bases = [[starts[p]] for p in range(n_parts)]
    lens = [[parts[p]] for p in range(n_parts)]

    def scatter_start(p, i):
        m, me, dev = orders[p][i]
        size = lens[p][i] // m
        src = in_ref if i == 0 else acc
        copies = []
        for d in range(1, m):
            q = (me + d) % m
            c = pltpu.make_async_remote_copy(
                src_ref=src.at[pl.ds(pl.multiple_of(bases[p][i] + q * size, 8), size)],
                dst_ref=recv[p][i].at[d - 1],
                send_sem=send_sem.at[p, i, d - 1],
                recv_sem=recv_sem.at[p, i, d - 1],
                device_id=dev(q),
                device_id_type=MESH,
            )
            c.start()
            copies.append(c)
        return copies

    def scatter_finish(p, i, copies):
        m, me, _ = orders[p][i]
        size = lens[p][i] // m
        base = pl.multiple_of(bases[p][i] + me * size, 8)
        src = in_ref if i == 0 else acc
        total = src[pl.ds(base, size)]
        for d in range(1, m):
            copies[d - 1].wait_recv()
            total = total + recv[p][i][d - 1]
        dst = out_ref if i == 2 else acc
        dst[pl.ds(base, size)] = total
        bases[p].append(base)
        lens[p].append(size)

    def gather_start(p, i):
        m, me, dev = orders[p][i]
        size = lens[p][i + 1]
        mine = out_ref.at[pl.ds(bases[p][i + 1], size)]
        copies = []
        for d in range(1, m):
            c = pltpu.make_async_remote_copy(
                src_ref=mine,
                dst_ref=mine,
                send_sem=send2.at[p, i, d - 1],
                recv_sem=recv2.at[p, i, d - 1],
                device_id=dev((me + d) % m),
                device_id_type=MESH,
            )
            c.start()
            copies.append(c)
        return copies

    sent = []
    live = [scatter_start(p, 0) for p in range(n_parts)]
    for i in range(3):
        for p in range(n_parts):
            scatter_finish(p, i, live[p])
            sent += live[p]
            live[p] = scatter_start(p, i + 1) if i < 2 else gather_start(p, 2)
    for i in (2, 1, 0):
        for p in range(n_parts):
            for c in live[p]:
                c.wait_recv()
            sent += live[p]
            live[p] = gather_start(p, i - 1) if i > 0 else []
    for c in sent:
        c.wait_send()


def all_reduce(blocks, n_grp, n_shard):
    n = n_grp * n_shard
    rows = blocks.shape[0]
    padded = -(-rows // (8 * n)) * (8 * n)
    if padded != rows:
        blocks = jnp.pad(blocks, ((0, padded - rows), (0, 0)))
    parts = split_rows(padded, n)
    sizes = phase_sizes(n_grp, n_shard, len(parts))
    most = max(max(m) for m in sizes)
    scratch = []
    for part, ms in zip(parts, sizes):
        size = part
        for m in ms:
            size //= m
            scratch.append(pltpu.VMEM((max(m - 1, 1), size, BLK), jnp.float32))
    sems = pltpu.SemaphoreType.DMA((len(parts), 3, max(most - 1, 1)))
    scratch += [pltpu.VMEM((padded, BLK), jnp.float32), sems, sems, sems, sems]
    return pl.pallas_call(
        functools.partial(reduce_kernel, n_grp, n_shard, parts),
        out_shape=jax.ShapeDtypeStruct((padded, BLK), jnp.float32),
        in_specs=[pl.BlockSpec(memory_space=pltpu.VMEM)],
        out_specs=pl.BlockSpec(memory_space=pltpu.VMEM),
        scratch_shapes=scratch,
        compiler_params=pltpu.CompilerParams(
            collective_id=0, has_side_effects=True, vmem_limit_bytes=40 * 2**20
        ),
        name="reduce_terms",
    )(blocks)


def invert_block(a):
    sub = lax.broadcasted_iota(jnp.int32, (GRP8, BLK), 0)
    lane8 = lax.broadcasted_iota(jnp.int32, (GRP8, BLK), 1)
    lane = lax.broadcasted_iota(jnp.int32, (BLK, BLK), 1)
    for g in range(BLK // GRP8):
        lo = g * GRP8
        cols = [
            jnp.broadcast_to(a[:, lo + c : lo + c + 1], (BLK, BLK)) for c in range(GRP8)
        ]
        own = [c[lo : lo + GRP8, :] for c in cols]
        inside = (lane8 >= lo) & (lane8 < lo + GRP8)
        r = jnp.where(
            inside, jnp.where(lane8 - lo == sub, 1.0, 0.0), a[lo : lo + GRP8, :]
        )
        for k in range(GRP8):
            at = sub == k
            pivot = jnp.broadcast_to(own[k][k : k + 1, :], (GRP8, BLK))
            mult = jnp.where(at, -1.0, own[k]) / pivot
            for c in range(k + 1, GRP8):
                row = jnp.broadcast_to(own[c][k : k + 1, :], (GRP8, BLK))
                own[c] = jnp.where(at, 0.0, own[c]) - mult * row
            row = jnp.broadcast_to(r[k : k + 1, :], (GRP8, BLK))
            r = jnp.where(at, 0.0, r) - mult * row
        rest = jnp.where((lane >= lo) & (lane < lo + GRP8), 0.0, a)
        for c in range(GRP8):
            rest = rest - cols[c] * jnp.broadcast_to(r[c : c + 1, :], (BLK, BLK))
        pieces = [rest[:lo]] * (lo > 0) + [r] + [rest[lo + GRP8 :]] * (lo + GRP8 < BLK)
        a = jnp.concatenate(pieces, axis=0)
    return a


def solve_kernel(
    nk, nt, tiles, b_ref, x_hbm, y_hbm, pred_ref, res_hbm,
    gram, cross, panel, high, low, xv, yv, ov, in_sem, out_sem,
):
    load_x = pltpu.make_async_copy(x_hbm, xv, in_sem.at[0])
    load_y = pltpu.make_async_copy(y_hbm, yv, in_sem.at[1])
    load_x.start()
    load_y.start()

    at = 0
    for i in range(nk):
        for j in range(i + 1):
            block = b_ref[at * BLK : (at + 1) * BLK, :]
            at += 1
            gram[i * BLK : (i + 1) * BLK, j * BLK : (j + 1) * BLK] = block
            if i != j:
                gram[j * BLK : (j + 1) * BLK, i * BLK : (i + 1) * BLK] = block.T
    for i in range(nk):
        for j in range(nt):
            cross[i * BLK : (i + 1) * BLK, j * BLK : (j + 1) * BLK] = b_ref[
                at * BLK : (at + 1) * BLK, :
            ]
            at += 1

    def stage(j, carry):
        here = pl.ds(pl.multiple_of(j * BLK, BLK), BLK)
        inverse = invert_block(gram[here, here])
        panel[...] = dot32(inverse, gram[here, :])
        panel[:, here] = inverse
        side = gram[:, here]
        gram[:, here] = jnp.zeros_like(side)
        gram[...] -= dot32(side, panel[...])
        gram[here, :] = panel[...]
        return carry

    lax.fori_loop(0, nk, stage, 0)
    pred = dot32(gram[...], cross[...])
    pred_ref[...] = pred
    top = pred.astype(jnp.bfloat16)
    high[...] = top
    low[...] = (pred - top.astype(jnp.float32)).astype(jnp.bfloat16)

    load_x.wait()
    load_y.wait()
    rows = xv.shape[0] // tiles
    stores = []
    for t in range(tiles):
        span = pl.ds(t * rows, rows)
        x = xv[span, :]
        estimate = jnp.dot(x, high[...], preferred_element_type=jnp.float32) + jnp.dot(
            x, low[...], preferred_element_type=jnp.float32
        )
        ov[span, :] = (yv[span, :].astype(jnp.float32) - estimate).astype(jnp.bfloat16)
        store = pltpu.make_async_copy(ov.at[span, :], res_hbm.at[span, :], out_sem.at[t])
        store.start()
        stores.append(store)
    for store in stores:
        store.wait()


def solve(total, regressors, targets):
    rows, k = regressors.shape
    p = targets.shape[1]
    tiles = 6 if rows % 96 == 0 else 1
    anywhere = pl.BlockSpec(memory_space=pl.ANY)
    in_vmem = pl.BlockSpec(memory_space=pltpu.VMEM)
    return pl.pallas_call(
        functools.partial(solve_kernel, k // BLK, p // BLK, tiles),
        out_shape=(
            jax.ShapeDtypeStruct((k, p), jnp.float32),
            jax.ShapeDtypeStruct((rows, p), jnp.bfloat16),
        ),
        in_specs=[in_vmem, anywhere, anywhere],
        out_specs=(in_vmem, anywhere),
        scratch_shapes=[
            pltpu.VMEM((k, k), jnp.float32),
            pltpu.VMEM((k, p), jnp.float32),
            pltpu.VMEM((BLK, k), jnp.float32),
            pltpu.VMEM((k, p), jnp.bfloat16),
            pltpu.VMEM((k, p), jnp.bfloat16),
            pltpu.VMEM((rows, k), jnp.bfloat16),
            pltpu.VMEM((rows, p), jnp.bfloat16),
            pltpu.VMEM((rows, p), jnp.bfloat16),
            pltpu.SemaphoreType.DMA((2,)),
            pltpu.SemaphoreType.DMA((tiles,)),
        ],
        compiler_params=pltpu.CompilerParams(vmem_limit_bytes=48 * 2**20),
        name="solve_and_residual",
    )(total, regressors, targets)


def body(n_grp, n_shard, regressors, targets):
    contract = (((0,), (0,)), ((), ()))
    gram = lax.dot_general(
        regressors, regressors, contract, preferred_element_type=jnp.float32
    )
    cross = lax.dot_general(
        regressors, targets, contract, preferred_element_type=jnp.float32
    )
    nk, nt = gram.shape[0] // BLK, cross.shape[1] // BLK

    def block(m, i, j):
        return m[i * BLK : (i + 1) * BLK, j * BLK : (j + 1) * BLK]

    blocks = [block(gram, i, j) for i in range(nk) for j in range(i + 1)]
    blocks += [block(cross, i, j) for i in range(nk) for j in range(nt)]
    total = all_reduce(jnp.concatenate(blocks, axis=0), n_grp, n_shard)
    return solve(total, regressors, targets)


def solution(mesh):
    placed = (P(("grp", "shard"), None), P(("grp", "shard"), None))
    return jax.shard_map(
        functools.partial(body, mesh.shape["grp"], mesh.shape["shard"]),
        mesh=mesh,
        in_specs=placed,
        out_specs=(P(), P(("grp", "shard"), None)),
        check_vma=False,
    )
```

time: 337 us -> 72.9 us (0.22)
  waiting for transfers between devices: 132 us -> 0 us
  other arithmetic: 125 us -> 0 us
  Pallas kernels: 0 us -> 65 us
  local copies, waits for them, and re-layouts: 30.5 us -> 0.29 us
  matrix products: 28.9 us -> 6.61 us
  between operations: 17.1 us -> 0.86 us
    psum x1 -> x0, waiting for transfers between devices: 132 us -> none  [body(): lax.psum((gram_local, cross_local), ('grp', 'shard'))]
    another operation x17 -> x0, other arithmetic: 123 us -> none  [the longest x14 80.4 us: body(): predictor = solve_predictor(jnp.linalg.cholesky(gram_total), cross_total)]
    pallas_call x0 -> x2, Pallas kernels: none -> 65 us  [the longest x1 34.2 us: all_reduce(): pl.pallas_call(functools.partial(reduce_kernel, n_grp, n_shard, parts), o...]
    another operation x20 -> x0, matrix products: 17.9 us -> none  [the longest x6 7.76 us: body(): predictor = solve_predictor(jnp.linalg.cholesky(gram_total), cross_total)]
    another operation x17 -> x0, local copies, waits for them, and re-layouts: 15.2 us -> none
    unnamed x14 -> x26, local copies, waits for them, and re-layouts: 12.7 us -> 0.28 us
    dot_general x2 -> x0, matrix products: 5.39 us -> none  [the longest x1 3.54 us: residual_block(): jnp.dot(rows_x, pred_low, preferred_element_type=jnp.float32)]
  transfers between devices with their start and end apart: 1 -> 0, of which waited for: 1 -> 0; matrix products, arithmetic and copies ran while one was open for 1% -> 0% of each run, Pallas kernels for 0% -> 0%
where the time goes in v1:
time: 72.9 us; the launch traced here: 72.7 us
  Pallas kernels  65 us (89%)
  matrix products  6.61 us (9%)
  between operations  0.86 us (1%)
    pallas_call x1, Pallas kernels, all_reduce(): pl.pallas_call(functools.partial(reduce_kernel, n_grp, n_shard, parts), o...  34.2 us
    pallas_call x1, Pallas kernels, solve(): pl.pallas_call(functools.partial(solve_kernel, k // BLK, p // BLK, tiles)...  30.7 us
    dot_general x1, matrix products, body(): lax.dot_general(regressors, targets, contract, preferred_element_type=jnp...  4.79 us
    dot_general x1, matrix products, body(): lax.dot_general(regressors, regressors, contract, preferred_element_type=...  1.82 us

profile of v1, /device:TPU:0, one launch (start us, length us, event | category | flops | bytes accessed | tf_op | source)
XLA Modules:
  0.0 72.7 jit_solution(17116725799467994556)
XLA Ops:
  0.6 0.0 copy-start
  0.6 4.8 %fusion.1 = f32[512,512]{1,0:T(8,128)S(1)} fusion(bf16[3072,512]{1,0:T(8,128)(2,1)} %x_hbm.1, bf16[3072,512]{1,0:T(8,128)(2,1)} %y_hbm.1), kind=kOutput, calls=%fused_computation.26 | convolution fusion | flops 1610612736 | bytes 7340032 | tf_op jit(solution)/shard_map/dot_general | solution.py:306
  5.4 0.0 copy-done
  5.4 1.8 %fusion = f32[512,512]{1,0:T(8,128)S(1)} fusion(bf16[3072,512]{1,0:T(8,128)(2,1)S(1)} %copy-done), kind=kOutput, calls=%fused_computation.25 | convolution fusion | flops 1610612736 | bytes 4194304 | tf_op jit(solution)/shard_map/dot_general | solution.py:303
  7.7 34.2 %reduce_terms.1.b_ref = f32[3328,128]{1,0:T(8,128)S(1)} custom-call(f32[3328,128]{1,0:T(8,128)S(1)} %slice_dynamic-update-slice_fusion.1.in_ref), custom_call_target="tpu_custom_call" | custom-call | tf_op jit(solution)/shard_map/reduce_terms/pallas_call | solution.py:166
  42.0 30.7 %solve_and_residual.1 = (f32[512,512]{1,0:T(8,128)}, bf16[3072,512]{1,0:T(8,128)(2,1)}) custom-call(f32[3328,128]{1,0:T(8,128)S(1)} %reduce_terms.1.b_ref, bf16[3072,512]{1,0:T(8,128)(2,1)S(1)} %copy-done, bf16[3072,512]{1,0:T(8,128)(2,1)} %y_hbm.1), custom_call_target="tpu_custom_call" | custom-call | tf_op jit(solution)/shard_map/solve_and_residual/pallas_call | solution.py:276
  (25 shorter events, 0.3 us)
Async XLA Ops:
  0.6 4.8 %copy-start = (bf16[3072,512]{1,0:T(8,128)(2,1)S(1)}, bf16[3072,512]{1,0:T(8,128)(2,1)}, u32[]{:S(2)}) copy-start(bf16[3072,512]{1,0:T(8,128)(2,1)} %x_hbm.1) | copy-start | bytes 9437188

commit v2 on v1

v2 whole, which is shorter than its diff:
```python
import functools

import jax
import jax.numpy as jnp
from jax import lax
from jax.experimental import pallas as pl
from jax.experimental.pallas import tpu as pltpu
from jax.sharding import PartitionSpec as P

MESH = pl.DeviceIdType.MESH
BLK = 128
GRP8 = 8
HIGHEST = lax.Precision.HIGHEST


def dot32(a, b):
    return jnp.dot(a, b, preferred_element_type=jnp.float32, precision=HIGHEST)


def phases(n_grp, n_shard):
    g, s = lax.axis_index("grp"), lax.axis_index("shard")
    cores = 2 if n_grp % 2 == 0 else 1
    ny = n_grp // cores
    nx = ny if n_shard % ny == 0 else 1
    nz = n_shard // nx
    y, core = g // cores, g % cores
    z, x = s // nx, s % nx
    core_ph = (cores, core, lambda q: (y * cores + q, s))
    plane_ph = (
        ny * nx,
        y * nx + x,
        lambda q: ((q // nx) * cores + core, z * nx + q % nx),
    )
    line_ph = (nz, z, lambda q: (g, q * nx + x))
    return core_ph, plane_ph, line_ph


def split_rows(rows, n):
    unit = 8 * n
    units = rows // unit
    if units < 2:
        return (rows,)
    first = max(1, (units * 2 + 1) // 3)
    return (first * unit, (units - first) * unit)


def phase_sizes(n_grp, n_shard, n_parts):
    cores = 2 if n_grp % 2 == 0 else 1
    ny = n_grp // cores
    nx = ny if n_shard % ny == 0 else 1
    nz = n_shard // nx
    return [(cores, ny * nx, nz), (cores, nz, ny * nx)][:n_parts]


class Sum:
    def __init__(self, src, out, parts, orders, scratch):
        self.src, self.out, self.orders = src, out, orders
        self.recv = [scratch[3 * p : 3 * p + 3] for p in range(len(parts))]
        self.acc, *self.sems = scratch[3 * len(parts) :]
        starts = [sum(parts[:p]) for p in range(len(parts))]
        self.bases, self.lens = [], []
        for start, rows, order in zip(starts, parts, orders):
            bases, lens = [start], [rows]
            for m, me, _ in order:
                lens.append(lens[-1] // m)
                bases.append(pl.multiple_of(bases[-1] + me * lens[-1], 8))
            self.bases.append(bases)
            self.lens.append(lens)
        self.n_parts = len(parts)

    def scatter(self, p, i):
        m, me, dev = self.orders[p][i]
        size = self.lens[p][i + 1]
        src = self.src if i == 0 else self.acc
        copies = []
        for d in range(1, m):
            q = (me + d) % m
            at = pl.multiple_of(self.bases[p][i] + q * size, 8)
            copies.append(
                pltpu.make_async_remote_copy(
                    src_ref=src.at[pl.ds(at, size)],
                    dst_ref=self.recv[p][i].at[d - 1],
                    send_sem=self.sems[0].at[p, i, d - 1],
                    recv_sem=self.sems[1].at[p, i, d - 1],
                    device_id=dev(q),
                    device_id_type=MESH,
                )
            )
        return copies

    def gather(self, p, i):
        m, me, dev = self.orders[p][i]
        mine = self.out.at[pl.ds(self.bases[p][i + 1], self.lens[p][i + 1])]
        return [
            pltpu.make_async_remote_copy(
                src_ref=mine,
                dst_ref=mine,
                send_sem=self.sems[2].at[p, i, d - 1],
                recv_sem=self.sems[3].at[p, i, d - 1],
                device_id=dev((me + d) % m),
                device_id_type=MESH,
            )
            for d in range(1, m)
        ]

    def add(self, p, i):
        copies = self.scatter(p, i)
        src = self.src if i == 0 else self.acc
        dst = self.out if i == 2 else self.acc
        span = pl.ds(self.bases[p][i + 1], self.lens[p][i + 1])
        total = src[span]
        for d, copy in enumerate(copies):
            copy.wait_recv()
            total = total + self.recv[p][i][d]
        dst[span] = total

    def step(self, t):
        for p in range(self.n_parts):
            if 1 <= t <= 3:
                self.add(p, t - 1)
            elif t > 3:
                for copy in self.gather(p, 6 - t):
                    copy.wait_recv()
            if t < 3:
                started = self.scatter(p, t)
            elif t < 6:
                started = self.gather(p, 5 - t)
            else:
                started = []
            for copy in started:
                copy.start()

    def finish(self):
        for p in range(self.n_parts):
            for i in range(3):
                for copy in self.scatter(p, i) + self.gather(p, i):
                    copy.wait_send()


def sum_scratch(rows, n_grp, n_shard):
    parts = split_rows(rows, n_grp * n_shard)
    sizes = phase_sizes(n_grp, n_shard, len(parts))
    most = max(max(m) for m in sizes)
    scratch = []
    for part, ms in zip(parts, sizes):
        size = part
        for m in ms:
            size //= m
            scratch.append(pltpu.VMEM((max(m - 1, 1), size, BLK), jnp.float32))
    sems = pltpu.SemaphoreType.DMA((len(parts), 3, max(most - 1, 1)))
    scratch += [pltpu.VMEM((rows, BLK), jnp.float32), sems, sems, sems, sems]
    return parts, scratch


def normal_kernel(
    n_grp, n_shard, nk, nt, g_parts, c_parts, gram_in, x_hbm, y_hbm,
    gram, cross_out, xv, yv, cross_in, gram_out, panel, in_sem, *scratch,
):
    load_x = pltpu.make_async_copy(x_hbm, xv, in_sem.at[0])
    load_y = pltpu.make_async_copy(y_hbm, yv, in_sem.at[1])
    load_x.start()
    load_y.start()

    a, b, c = phases(n_grp, n_shard)
    barrier = pltpu.get_barrier_semaphore()
    count = 0
    for m, me, dev in (a, b, c):
        for d in range(1, m):
            pl.semaphore_signal(
                barrier, inc=1, device_id=dev((me + d) % m), device_id_type=MESH
            )
            count += 1
    pl.semaphore_wait(barrier, count)

    orders = [(a, b, c), (a, c, b)]
    n_first = 3 * len(g_parts) + 5
    gsum = Sum(gram_in, gram_out, g_parts, orders[: len(g_parts)], scratch[:n_first])
    csum = Sum(cross_in, cross_out, c_parts, orders[: len(c_parts)], scratch[n_first:])

    gsum.step(0)
    gsum.step(1)
    load_x.wait()
    load_y.wait()
    used = nk * nt * BLK
    if used < cross_in.shape[0]:
        cross_in[used:, :] = jnp.zeros((cross_in.shape[0] - used, BLK), jnp.float32)
    wide = 2 if nt % 2 == 0 else 1

    def cross_columns(j):
        part = lax.dot_general(
            xv[...],
            yv[:, j * BLK : (j + wide) * BLK],
            (((0,), (0,)), ((), ())),
            preferred_element_type=jnp.float32,
        )
        for w in range(wide):
            cross_in[(j + w) * nk * BLK : (j + w + 1) * nk * BLK, :] = part[
                :, w * BLK : (w + 1) * BLK
            ]

    columns = list(range(0, nt, wide))
    for j in columns[: len(columns) // 2]:
        cross_columns(j)
    gsum.step(2)
    for j in columns[len(columns) // 2 :]:
        cross_columns(j)
    gsum.step(3)
    csum.step(0)
    for t in (4, 5, 6):
        gsum.step(t)

    at = 0
    for i in range(nk):
        for j in range(i + 1):
            block = gram_out[at * BLK : (at + 1) * BLK, :]
            at += 1
            gram[i * BLK : (i + 1) * BLK, j * BLK : (j + 1) * BLK] = block
            if i != j:
                gram[j * BLK : (j + 1) * BLK, i * BLK : (i + 1) * BLK] = block.T
    csum.step(1)

    def stage(j, carry):
        here = pl.ds(pl.multiple_of(j * BLK, BLK), BLK)
        inverse = invert_block(gram[here, here])
        for t in range(min(nk, 5)):
            @pl.when(j == t)
            def _(t=t):
                csum.step(t + 2)

        panel[...] = dot32(inverse, gram[here, :])
        panel[:, here] = inverse
        side = gram[:, here]
        gram[:, here] = jnp.zeros_like(side)
        gram[...] -= dot32(side, panel[...])
        gram[here, :] = panel[...]
        return carry

    lax.fori_loop(0, nk, stage, 0)
    for t in range(min(nk, 5) + 2, 7):
        csum.step(t)
    gsum.finish()
    csum.finish()


def normal_equations(blocks, regressors, targets, n_grp, n_shard):
    rows, k = regressors.shape
    p = targets.shape[1]
    nk, nt = k // BLK, p // BLK
    unit = 8 * n_grp * n_shard
    padded = -(-blocks.shape[0] // unit) * unit
    if padded != blocks.shape[0]:
        blocks = jnp.pad(blocks, ((0, padded - blocks.shape[0]), (0, 0)))
    cross_rows = -(-(nk * nt * BLK) // unit) * unit
    g_parts, g_scratch = sum_scratch(padded, n_grp, n_shard)
    c_parts, c_scratch = sum_scratch(cross_rows, n_grp, n_shard)
    anywhere = pl.BlockSpec(memory_space=pl.ANY)
    in_vmem = pl.BlockSpec(memory_space=pltpu.VMEM)
    return pl.pallas_call(
        functools.partial(normal_kernel, n_grp, n_shard, nk, nt, g_parts, c_parts),
        out_shape=(
            jax.ShapeDtypeStruct((k, k), jnp.float32),
            jax.ShapeDtypeStruct((cross_rows, BLK), jnp.float32),
        ),
        in_specs=[in_vmem, anywhere, anywhere],
        out_specs=(in_vmem, in_vmem),
        scratch_shapes=[
            pltpu.VMEM((rows, k), jnp.bfloat16),
            pltpu.VMEM((rows, p), jnp.bfloat16),
            pltpu.VMEM((cross_rows, BLK), jnp.float32),
            pltpu.VMEM((padded, BLK), jnp.float32),
            pltpu.VMEM((BLK, k), jnp.float32),
            pltpu.SemaphoreType.DMA((2,)),
            *g_scratch,
            *c_scratch,
        ],
        compiler_params=pltpu.CompilerParams(
            collective_id=0, has_side_effects=True, vmem_limit_bytes=44 * 2**20
        ),
        name="normal_equations",
    )(blocks, regressors, targets)


def reciprocal(p):
    r = pl.reciprocal(p, approx=True)
    r = r * (2.0 - p * r)
    return r * (2.0 - p * r)


def invert_block(a):
    sub = lax.broadcasted_iota(jnp.int32, (GRP8, BLK), 0)
    lane8 = lax.broadcasted_iota(jnp.int32, (GRP8, BLK), 1)
    lane = lax.broadcasted_iota(jnp.int32, (BLK, BLK), 1)
    for g in range(BLK // GRP8):
        lo = g * GRP8
        cols = [
            jnp.broadcast_to(a[:, lo + c : lo + c + 1], (BLK, BLK)) for c in range(GRP8)
        ]
        own = [c[lo : lo + GRP8, :] for c in cols]
        inside = (lane8 >= lo) & (lane8 < lo + GRP8)
        r = jnp.where(
            inside, jnp.where(lane8 - lo == sub, 1.0, 0.0), a[lo : lo + GRP8, :]
        )
        for k in range(GRP8):
            at = sub == k
            pivot = jnp.broadcast_to(own[k][k : k + 1, :], (GRP8, BLK))
            mult = jnp.where(at, -1.0, own[k]) * reciprocal(pivot)
            for c in range(k + 1, GRP8):
                row = jnp.broadcast_to(own[c][k : k + 1, :], (GRP8, BLK))
                own[c] = jnp.where(at, 0.0, own[c]) - mult * row
            row = jnp.broadcast_to(r[k : k + 1, :], (GRP8, BLK))
            r = jnp.where(at, 0.0, r) - mult * row
        rest = jnp.where((lane >= lo) & (lane < lo + GRP8), 0.0, a)
        for c in range(GRP8):
            rest = rest - cols[c] * jnp.broadcast_to(r[c : c + 1, :], (BLK, BLK))
        pieces = [rest[:lo]] * (lo > 0) + [r] + [rest[lo + GRP8 :]] * (lo + GRP8 < BLK)
        a = jnp.concatenate(pieces, axis=0)
    return a


def solve_kernel(
    nk, nt, tiles, inv_ref, b_ref, x_hbm, y_hbm, pred_ref, res_hbm,
    cross, high, low, xv, yv, ov, in_sem, out_sem,
):
    load_x = pltpu.make_async_copy(x_hbm, xv, in_sem.at[0])
    load_y = pltpu.make_async_copy(y_hbm, yv, in_sem.at[1])
    load_x.start()
    load_y.start()

    depth = nk * BLK
    for j in range(nt):
        cross[:, j * BLK : (j + 1) * BLK] = b_ref[j * depth : (j + 1) * depth, :]
    pred = dot32(inv_ref[...], cross[...])
    pred_ref[...] = pred
    top = pred.astype(jnp.bfloat16)
    high[...] = top
    low[...] = (pred - top.astype(jnp.float32)).astype(jnp.bfloat16)

    load_x.wait()
    load_y.wait()
    rows = xv.shape[0] // tiles
    stores = []
    for t in range(tiles):
        span = pl.ds(t * rows, rows)
        x = xv[span, :]
        estimate = jnp.dot(x, high[...], preferred_element_type=jnp.float32) + jnp.dot(
            x, low[...], preferred_element_type=jnp.float32
        )
        ov[span, :] = (yv[span, :].astype(jnp.float32) - estimate).astype(jnp.bfloat16)
        store = pltpu.make_async_copy(ov.at[span, :], res_hbm.at[span, :], out_sem.at[t])
        store.start()
        stores.append(store)
    for store in stores:
        store.wait()


def solve(inverse, total, regressors, targets):
    rows, k = regressors.shape
    p = targets.shape[1]
    tiles = 6 if rows % 96 == 0 else 1
    anywhere = pl.BlockSpec(memory_space=pl.ANY)
    in_vmem = pl.BlockSpec(memory_space=pltpu.VMEM)
    return pl.pallas_call(
        functools.partial(solve_kernel, k // BLK, p // BLK, tiles),
        out_shape=(
            jax.ShapeDtypeStruct((k, p), jnp.float32),
            jax.ShapeDtypeStruct((rows, p), jnp.bfloat16),
        ),
        in_specs=[in_vmem, in_vmem, anywhere, anywhere],
        out_specs=(in_vmem, anywhere),
        scratch_shapes=[
            pltpu.VMEM((k, p), jnp.float32),
            pltpu.VMEM((k, p), jnp.bfloat16),
            pltpu.VMEM((k, p), jnp.bfloat16),
            pltpu.VMEM((rows, k), jnp.bfloat16),
            pltpu.VMEM((rows, p), jnp.bfloat16),
            pltpu.VMEM((rows, p), jnp.bfloat16),
            pltpu.SemaphoreType.DMA((2,)),
            pltpu.SemaphoreType.DMA((tiles,)),
        ],
        compiler_params=pltpu.CompilerParams(vmem_limit_bytes=48 * 2**20),
        name="solve_and_residual",
    )(inverse, total, regressors, targets)


def body(n_grp, n_shard, regressors, targets):
    contract = (((0,), (0,)), ((), ()))
    gram = lax.dot_general(
        regressors, regressors, contract, preferred_element_type=jnp.float32
    )
    nk = gram.shape[0] // BLK

    def block(i, j):
        return gram[i * BLK : (i + 1) * BLK, j * BLK : (j + 1) * BLK]

    blocks = jnp.concatenate(
        [block(i, j) for i in range(nk) for j in range(i + 1)], axis=0
    )
    inverse, total = normal_equations(blocks, regressors, targets, n_grp, n_shard)
    return solve(inverse, total, regressors, targets)


def solution(mesh):
    placed = (P(("grp", "shard"), None), P(("grp", "shard"), None))
    return jax.shard_map(
        functools.partial(body, mesh.shape["grp"], mesh.shape["shard"]),
        mesh=mesh,
        in_specs=placed,
        out_specs=(P(), P(("grp", "shard"), None)),
        check_vma=False,
    )
```

time: 72.9 us -> 70.8 us (0.971)
  matrix products: 6.61 us -> 4.79 us
    pallas_call x1, Pallas kernels: 34.2 us -> 56.6 us  [normal_equations(): pl.pallas_call(functools.partial(normal_kernel, n_grp, n_shard, nk, nt, g...]
    pallas_call x1, Pallas kernels: 30.7 us -> 8.38 us  [solve(): pl.pallas_call(functools.partial(solve_kernel, k // BLK, p // BLK, tiles)...]
    dot_general x1 -> x0, matrix products: 4.79 us -> none  [body(): lax.dot_general(regressors, targets, contract, preferred_element_type=jnp...]
    dot_general x1, matrix products: 1.82 us -> 4.79 us  [body(): lax.dot_general(regressors, regressors, contract, preferred_element_type=...]
where the time goes in v2:
time: 70.8 us; the launch traced here: 70.6 us
  Pallas kernels  65 us (92%)
  matrix products  4.79 us (7%)
  between operations  0.74 us (1%)
    pallas_call x1, Pallas kernels, normal_equations(): pl.pallas_call(functools.partial(normal_kernel, n_grp, n_shard, nk, nt, g...  56.6 us
    pallas_call x1, Pallas kernels, solve(): pl.pallas_call(functools.partial(solve_kernel, k // BLK, p // BLK, tiles)...  8.38 us
    dot_general x1, matrix products, body(): lax.dot_general(regressors, regressors, contract, preferred_element_type=...  4.79 us

profile of v2, /device:TPU:0, one launch (start us, length us, event | category | flops | bytes accessed | tf_op | source)
XLA Modules:
  0.0 70.6 jit_solution(7629009108281007723)
XLA Ops:
  0.6 0.0 copy-start
  0.6 0.0 copy-start.1
  0.7 4.8 %fusion = f32[512,512]{1,0:T(8,128)S(1)} fusion(bf16[3072,512]{1,0:T(8,128)(2,1)} %x_hbm.3), kind=kOutput, calls=%fused_computation.9 | convolution fusion | flops 1610612736 | bytes 4194304 | tf_op jit(solution)/shard_map/dot_general | solution.py:387
  5.6 0.0 copy-done
  5.6 0.0 copy-done.1
  5.6 56.6 %normal_equations.1 = (f32[512,512]{1,0:T(8,128)S(1)}, f32[2048,128]{1,0:T(8,128)S(1)}) custom-call(f32[1280,128]{1,0:T(8,128)S(1)} %slice_dynamic-update-slice_fusion.1.gram_in, bf16[3072,512]{1,0:T(8,128)(2,1)S(1)} %copy-done, bf16[3072,512]{1,0:T(8,128)(2,1)S(1)} %copy-done.1), custom_call_target="tpu_custom_call" | custom-call | tf_op jit(solution)/shard_map/normal_equations/pallas_call | solution.py:258
  62.3 8.4 %solve_and_residual.1 = (f32[512,512]{1,0:T(8,128)}, bf16[3072,512]{1,0:T(8,128)(2,1)}) custom-call(f32[512,512]{1,0:T(8,128)S(1)} %get-tuple-element.4.inv_ref, f32[2048,128]{1,0:T(8,128)S(1)} %get-tuple-element.5.b_ref, bf16[3072,512]{1,0:T(8,128)(2,1)S(1)} %copy-done, bf16[3072,512]{1,0:T(8,128)(2,1)} %y_hbm.3), custom_call_target="tpu_custom_call" | custom-call | tf_op jit(solution)/shard_map/solve_and_residual/pallas_call | solution.py:362
  (9 shorter events, 0.1 us)
Async XLA Ops:
  0.6 5.0 %copy-start = (bf16[3072,512]{1,0:T(8,128)(2,1)S(1)}, bf16[3072,512]{1,0:T(8,128)(2,1)}, u32[]{:S(2)}) copy-start(bf16[3072,512]{1,0:T(8,128)(2,1)} %x_hbm.3) | copy-start | bytes 9437188
  0.6 5.0 %copy-start.1 = (bf16[3072,512]{1,0:T(8,128)(2,1)S(1)}, bf16[3072,512]{1,0:T(8,128)(2,1)}, u32[]{:S(2)}) copy-start(bf16[3072,512]{1,0:T(8,128)(2,1)} %y_hbm.3) | copy-start | bytes 9437188

commit v3 on v2

--- a/solution.py
+++ b/solution.py
@@ -153,14 +153,9 @@
 
 
 def normal_kernel(
-    n_grp, n_shard, nk, nt, g_parts, c_parts, gram_in, x_hbm, y_hbm,
-    gram, cross_out, xv, yv, cross_in, gram_out, panel, in_sem, *scratch,
+    n_grp, n_shard, nk, g_parts, c_parts, gram_in, cross_in,
+    gram, cross_out, gram_out, panel, *scratch,
 ):
-    load_x = pltpu.make_async_copy(x_hbm, xv, in_sem.at[0])
-    load_y = pltpu.make_async_copy(y_hbm, yv, in_sem.at[1])
-    load_x.start()
-    load_y.start()
-
     a, b, c = phases(n_grp, n_shard)
     barrier = pltpu.get_barrier_semaphore()
     count = 0
@@ -179,41 +174,25 @@
 
     gsum.step(0)
     gsum.step(1)
-    load_x.wait()
-    load_y.wait()
-    used = nk * nt * BLK
-    if used < cross_in.shape[0]:
-        cross_in[used:, :] = jnp.zeros((cross_in.shape[0] - used, BLK), jnp.float32)
-    wide = 2 if nt % 2 == 0 else 1
-
-    def cross_columns(j):
-        part = lax.dot_general(
-            xv[...],
-            yv[:, j * BLK : (j + wide) * BLK],
-            (((0,), (0,)), ((), ())),
-            preferred_element_type=jnp.float32,
-        )
-        for w in range(wide):
-            cross_in[(j + w) * nk * BLK : (j + w + 1) * nk * BLK, :] = part[
-                :, w * BLK : (w + 1) * BLK
-            ]
-
-    columns = list(range(0, nt, wide))
-    for j in columns[: len(columns) // 2]:
-        cross_columns(j)
     gsum.step(2)
-    for j in columns[len(columns) // 2 :]:
-        cross_columns(j)
     gsum.step(3)
     csum.step(0)
     for t in (4, 5, 6):
         gsum.step(t)
 
-    at = 0
+    eye = lax.broadcasted_iota(jnp.int32, (BLK, BLK), 0) == lax.broadcasted_iota(
+        jnp.int32, (BLK, BLK), 1
+    )
+    down, across = [], []
+    for i in range(nk):
+        at = i * (i + 1) // 2 + i
+        diagonal = jnp.where(eye, gram_out[at * BLK : (at + 1) * BLK, :], 0.0)
+        down.append(lax.rsqrt(jnp.sum(diagonal, axis=1, keepdims=True)))
+        across.append(lax.rsqrt(jnp.sum(diagonal, axis=0, keepdims=True)))
     for i in range(nk):
         for j in range(i + 1):
-            block = gram_out[at * BLK : (at + 1) * BLK, :]
-            at += 1
+            at = i * (i + 1) // 2 + j
+            block = gram_out[at * BLK : (at + 1) * BLK, :] * down[i] * across[j]
             gram[i * BLK : (i + 1) * BLK, j * BLK : (j + 1) * BLK] = block
             if i != j:
                 gram[j * BLK : (j + 1) * BLK, i * BLK : (i + 1) * BLK] = block.T
@@ -236,40 +215,40 @@
         return carry
 
     lax.fori_loop(0, nk, stage, 0)
+    for i in range(nk):
+        for j in range(nk):
+            gram[i * BLK : (i + 1) * BLK, j * BLK : (j + 1) * BLK] *= down[i] * across[j]
     for t in range(min(nk, 5) + 2, 7):
         csum.step(t)
     gsum.finish()
     csum.finish()
 
 
-def normal_equations(blocks, regressors, targets, n_grp, n_shard):
-    rows, k = regressors.shape
-    p = targets.shape[1]
-    nk, nt = k // BLK, p // BLK
+def padded_rows(blocks, unit):
+    extra = -blocks.shape[0] % unit
+    return jnp.pad(blocks, ((0, extra), (0, 0))) if extra else blocks
+
+
+def normal_equations(gram_blocks, cross_blocks, k, n_grp, n_shard):
+    nk = k // BLK
     unit = 8 * n_grp * n_shard
-    padded = -(-blocks.shape[0] // unit) * unit
-    if padded != blocks.shape[0]:
-        blocks = jnp.pad(blocks, ((0, padded - blocks.shape[0]), (0, 0)))
-    cross_rows = -(-(nk * nt * BLK) // unit) * unit
+    gram_blocks = padded_rows(gram_blocks, unit)
+    cross_blocks = padded_rows(cross_blocks, unit)
+    padded, cross_rows = gram_blocks.shape[0], cross_blocks.shape[0]
     g_parts, g_scratch = sum_scratch(padded, n_grp, n_shard)
     c_parts, c_scratch = sum_scratch(cross_rows, n_grp, n_shard)
-    anywhere = pl.BlockSpec(memory_space=pl.ANY)
     in_vmem = pl.BlockSpec(memory_space=pltpu.VMEM)
     return pl.pallas_call(
-        functools.partial(normal_kernel, n_grp, n_shard, nk, nt, g_parts, c_parts),
+        functools.partial(normal_kernel, n_grp, n_shard, nk, g_parts, c_parts),
         out_shape=(
             jax.ShapeDtypeStruct((k, k), jnp.float32),
             jax.ShapeDtypeStruct((cross_rows, BLK), jnp.float32),
         ),
-        in_specs=[in_vmem, anywhere, anywhere],
+        in_specs=[in_vmem, in_vmem],
         out_specs=(in_vmem, in_vmem),
         scratch_shapes=[
-            pltpu.VMEM((rows, k), jnp.bfloat16),
-            pltpu.VMEM((rows, p), jnp.bfloat16),
-            pltpu.VMEM((cross_rows, BLK), jnp.float32),
             pltpu.VMEM((padded, BLK), jnp.float32),
             pltpu.VMEM((BLK, k), jnp.float32),
-            pltpu.SemaphoreType.DMA((2,)),
             *g_scratch,
             *c_scratch,
         ],
@@ -277,7 +256,7 @@
             collective_id=0, has_side_effects=True, vmem_limit_bytes=44 * 2**20
         ),
         name="normal_equations",
-    )(blocks, regressors, targets)
+    )(gram_blocks, cross_blocks)
 
 
 def reciprocal(p):
@@ -300,18 +279,33 @@
         r = jnp.where(
             inside, jnp.where(lane8 - lo == sub, 1.0, 0.0), a[lo : lo + GRP8, :]
         )
-        for k in range(GRP8):
-            at = sub == k
-            pivot = jnp.broadcast_to(own[k][k : k + 1, :], (GRP8, BLK))
-            mult = jnp.where(at, -1.0, own[k]) * reciprocal(pivot)
-            for c in range(k + 1, GRP8):
-                row = jnp.broadcast_to(own[c][k : k + 1, :], (GRP8, BLK))
-                own[c] = jnp.where(at, 0.0, own[c]) - mult * row
-            row = jnp.broadcast_to(r[k : k + 1, :], (GRP8, BLK))
-            r = jnp.where(at, 0.0, r) - mult * row
+        def spread(t, k):
+            return jnp.broadcast_to(t[k : k + 1, :], (GRP8, BLK))
+
+        for k in range(0, GRP8, 2):
+            first, second = sub == k, sub == k + 1
+            u, v = own[k], own[k + 1]
+            p00, p01 = spread(u, k), spread(v, k)
+            p10, p11 = spread(u, k + 1), spread(v, k + 1)
+            scale = reciprocal(p00 * p11 - p01 * p10)
+            m0 = jnp.where(first, -p11, jnp.where(second, p10, u * p11 - v * p10))
+            m1 = jnp.where(first, p01, jnp.where(second, -p00, v * p00 - u * p01))
+            pivots = first | second
+
+            def eliminate(t):
+                change = m0 * spread(t, k) + m1 * spread(t, k + 1)
+                return jnp.where(pivots, 0.0, t) - change * scale
+
+            for c in range(k + 2, GRP8):
+                own[c] = eliminate(own[c])
+            r = eliminate(r)
         rest = jnp.where((lane >= lo) & (lane < lo + GRP8), 0.0, a)
-        for c in range(GRP8):
-            rest = rest - cols[c] * jnp.broadcast_to(r[c : c + 1, :], (BLK, BLK))
+        terms = [
+            cols[c] * jnp.broadcast_to(r[c : c + 1, :], (BLK, BLK)) for c in range(GRP8)
+        ]
+        while len(terms) > 1:
+            terms = [terms[i] + terms[i + 1] for i in range(0, len(terms), 2)]
+        rest = rest - terms[0]
         pieces = [rest[:lo]] * (lo > 0) + [r] + [rest[lo + GRP8 :]] * (lo + GRP8 < BLK)
         a = jnp.concatenate(pieces, axis=0)
     return a
@@ -319,7 +313,7 @@
 
 def solve_kernel(
     nk, nt, tiles, inv_ref, b_ref, x_hbm, y_hbm, pred_ref, res_hbm,
-    cross, high, low, xv, yv, ov, in_sem, out_sem,
+    cross, both, xv, yv, ov, in_sem, out_sem,
 ):
     load_x = pltpu.make_async_copy(x_hbm, xv, in_sem.at[0])
     load_y = pltpu.make_async_copy(y_hbm, yv, in_sem.at[1])
@@ -332,8 +326,8 @@
     pred = dot32(inv_ref[...], cross[...])
     pred_ref[...] = pred
     top = pred.astype(jnp.bfloat16)
-    high[...] = top
-    low[...] = (pred - top.astype(jnp.float32)).astype(jnp.bfloat16)
+    both[:depth, :] = top
+    both[depth:, :] = (pred - top.astype(jnp.float32)).astype(jnp.bfloat16)
 
     load_x.wait()
     load_y.wait()
@@ -342,8 +336,8 @@
     for t in range(tiles):
         span = pl.ds(t * rows, rows)
         x = xv[span, :]
-        estimate = jnp.dot(x, high[...], preferred_element_type=jnp.float32) + jnp.dot(
-            x, low[...], preferred_element_type=jnp.float32
+        estimate = jnp.dot(
+            jnp.concatenate([x, x], axis=1), both[...], preferred_element_type=jnp.float32
         )
         ov[span, :] = (yv[span, :].astype(jnp.float32) - estimate).astype(jnp.bfloat16)
         store = pltpu.make_async_copy(ov.at[span, :], res_hbm.at[span, :], out_sem.at[t])
@@ -369,8 +363,7 @@
         out_specs=(in_vmem, anywhere),
         scratch_shapes=[
             pltpu.VMEM((k, p), jnp.float32),
-            pltpu.VMEM((k, p), jnp.bfloat16),
-            pltpu.VMEM((k, p), jnp.bfloat16),
+            pltpu.VMEM((2 * k, p), jnp.bfloat16),
             pltpu.VMEM((rows, k), jnp.bfloat16),
             pltpu.VMEM((rows, p), jnp.bfloat16),
             pltpu.VMEM((rows, p), jnp.bfloat16),
@@ -387,15 +380,22 @@
     gram = lax.dot_general(
         regressors, regressors, contract, preferred_element_type=jnp.float32
     )
-    nk = gram.shape[0] // BLK
+    cross = lax.dot_general(
+        regressors, targets, contract, preferred_element_type=jnp.float32
+    )
+    k = gram.shape[0]
+    nk, nt = k // BLK, cross.shape[1] // BLK
 
     def block(i, j):
         return gram[i * BLK : (i + 1) * BLK, j * BLK : (j + 1) * BLK]
 
-    blocks = jnp.concatenate(
+    gram_blocks = jnp.concatenate(
         [block(i, j) for i in range(nk) for j in range(i + 1)], axis=0
     )
-    inverse, total = normal_equations(blocks, regressors, targets, n_grp, n_shard)
+    cross_blocks = jnp.concatenate(
+        [cross[:, j * BLK : (j + 1) * BLK] for j in range(nt)], axis=0
+    )
+    inverse, total = normal_equations(gram_blocks, cross_blocks, k, n_grp, n_shard)
     return solve(inverse, total, regressors, targets)
 
 

time: 70.8 us -> 69.7 us (0.984)
  Pallas kernels: 65 us -> 61.8 us
  matrix products: 4.79 us -> 6.6 us
    pallas_call x1, Pallas kernels: 56.6 us -> 53.4 us  [normal_equations(): pl.pallas_call(functools.partial(normal_kernel, n_grp, n_shard, nk, g_par...]
    dot_general x0 -> x1, matrix products: none -> 1.81 us  [body(): lax.dot_general(regressors, targets, contract, preferred_element_type=jnp...]
where the time goes in v3:
time: 69.7 us; the launch traced here: 69.5 us
  Pallas kernels  61.8 us (89%)
  matrix products  6.6 us (9%)
  between operations  0.92 us (1%)
    pallas_call x1, Pallas kernels, normal_equations(): pl.pallas_call(functools.partial(normal_kernel, n_grp, n_shard, nk, g_par...  53.4 us
    pallas_call x1, Pallas kernels, solve(): pl.pallas_call(functools.partial(solve_kernel, k // BLK, p // BLK, tiles)...  8.38 us
    dot_general x1, matrix products, body(): lax.dot_general(regressors, regressors, contract, preferred_element_type=...  4.8 us
    dot_general x1, matrix products, body(): lax.dot_general(regressors, targets, contract, preferred_element_type=jnp...  1.81 us

profile of v3, /device:TPU:0, one launch (start us, length us, event | category | flops | bytes accessed | tf_op | source)
XLA Modules:
  0.0 69.5 jit_solution(5236155483616213980)
XLA Ops:
  0.6 0.0 copy-start
  0.6 0.0 copy-start.1
  0.7 4.8 %fusion.1 = f32[512,512]{1,0:T(8,128)S(1)} fusion(bf16[3072,512]{1,0:T(8,128)(2,1)} %x_hbm.1), kind=kOutput, calls=%fused_computation.11 | convolution fusion | flops 1610612736 | bytes 4194304 | tf_op jit(solution)/shard_map/dot_general | solution.py:380
  5.6 0.0 copy-done
  5.6 0.0 copy-done.1
  5.6 1.8 %fusion.2 = f32[512,512]{1,0:T(8,128)S(1)} fusion(bf16[3072,512]{1,0:T(8,128)(2,1)S(1)} %copy-done, bf16[3072,512]{1,0:T(8,128)(2,1)S(1)} %copy-done.1), kind=kOutput, calls=%fused_computation.12 | convolution fusion | flops 1610612736 | bytes 7340032 | tf_op jit(solution)/shard_map/dot_general | solution.py:383
  7.5 0.1 fusion
  7.5 0.1 pad_maximum_fusion.cross_in
  7.6 53.4 %normal_equations.1 = (f32[512,512]{1,0:T(8,128)S(1)}, f32[2048,128]{1,0:T(8,128)S(1)}) custom-call(f32[1280,128]{1,0:T(8,128)S(1)} %slice_dynamic-update-slice_fusion.1.gram_in, f32[2048,128]{1,0:T(8,128)S(1)} %pad_maximum_fusion.cross_in), custom_call_target="tpu_custom_call" | custom-call | tf_op jit(solution)/shard_map/normal_equations/pallas_call | solution.py:241
  61.0 8.4 %solve_and_residual.1 = (f32[512,512]{1,0:T(8,128)}, bf16[3072,512]{1,0:T(8,128)(2,1)}) custom-call(f32[512,512]{1,0:T(8,128)S(1)} %get-tuple-element.4.inv_ref, f32[2048,128]{1,0:T(8,128)S(1)} %get-tuple-element.5.b_ref, bf16[3072,512]{1,0:T(8,128)(2,1)S(1)} %copy-done, bf16[3072,512]{1,0:T(8,128)(2,1)} %y_hbm.1), custom_call_target="tpu_custom_call" | custom-call | tf_op jit(solution)/shard_map/solve_and_residual/pallas_call | solution.py:356
  (9 shorter events, 0.1 us)
Async XLA Ops:
  0.6 5.0 %copy-start = (bf16[3072,512]{1,0:T(8,128)(2,1)S(1)}, bf16[3072,512]{1,0:T(8,128)(2,1)}, u32[]{:S(2)}) copy-start(bf16[3072,512]{1,0:T(8,128)(2,1)} %x_hbm.1) | copy-start | bytes 9437188
  0.6 5.0 %copy-start.1 = (bf16[3072,512]{1,0:T(8,128)(2,1)S(1)}, bf16[3072,512]{1,0:T(8,128)(2,1)}, u32[]{:S(2)}) copy-start(bf16[3072,512]{1,0:T(8,128)(2,1)} %y_hbm.1) | copy-start | bytes 9437188

commit v4 on v3

--- a/solution.py
+++ b/solution.py
@@ -173,12 +173,13 @@
     csum = Sum(cross_in, cross_out, c_parts, orders[: len(c_parts)], scratch[n_first:])
 
     gsum.step(0)
+    csum.step(0)
     gsum.step(1)
     gsum.step(2)
-    gsum.step(3)
-    csum.step(0)
-    for t in (4, 5, 6):
+    csum.step(1)
+    for t in (3, 4, 5, 6):
         gsum.step(t)
+    csum.step(2)
 
     eye = lax.broadcasted_iota(jnp.int32, (BLK, BLK), 0) == lax.broadcasted_iota(
         jnp.int32, (BLK, BLK), 1
@@ -196,15 +197,14 @@
             gram[i * BLK : (i + 1) * BLK, j * BLK : (j + 1) * BLK] = block
             if i != j:
                 gram[j * BLK : (j + 1) * BLK, i * BLK : (i + 1) * BLK] = block.T
-    csum.step(1)
 
     def stage(j, carry):
         here = pl.ds(pl.multiple_of(j * BLK, BLK), BLK)
         inverse = invert_block(gram[here, here])
-        for t in range(min(nk, 5)):
+        for t in range(min(nk, 4)):
             @pl.when(j == t)
             def _(t=t):
-                csum.step(t + 2)
+                csum.step(t + 3)
 
         panel[...] = dot32(inverse, gram[here, :])
         panel[:, here] = inverse
@@ -218,7 +218,7 @@
     for i in range(nk):
         for j in range(nk):
             gram[i * BLK : (i + 1) * BLK, j * BLK : (j + 1) * BLK] *= down[i] * across[j]
-    for t in range(min(nk, 5) + 2, 7):
+    for t in range(min(nk, 4) + 3, 7):
         csum.step(t)
     gsum.finish()
     csum.finish()

time: 69.7 us -> 70.1 us (level); the launches traced: 69.5 us -> 69.1 us
  no operation moved by 1% of the time
where the time goes in v4:
time: 70.1 us; the launch traced here: 69.1 us
  Pallas kernels  61.3 us (87%)
  matrix products  6.6 us (9%)
  between operations  0.92 us (1%)
    pallas_call x1, Pallas kernels, normal_equations(): pl.pallas_call(functools.partial(normal_kernel, n_grp, n_shard, nk, g_par...  52.9 us
    pallas_call x1, Pallas kernels, solve(): pl.pallas_call(functools.partial(solve_kernel, k // BLK, p // BLK, tiles)...  8.38 us
    dot_general x1, matrix products, body(): lax.dot_general(regressors, regressors, contract, preferred_element_type=...  4.8 us
    dot_general x1, matrix products, body(): lax.dot_general(regressors, targets, contract, preferred_element_type=jnp...  1.81 us

profile of v4, /device:TPU:0, one launch (start us, length us, event | category | flops | bytes accessed | tf_op | source)
XLA Modules:
  0.0 69.1 jit_solution(9215983551726894473)
XLA Ops:
  0.6 0.0 copy-start
  0.6 0.0 copy-start.1
  0.7 4.8 %fusion.1 = f32[512,512]{1,0:T(8,128)S(1)} fusion(bf16[3072,512]{1,0:T(8,128)(2,1)} %x_hbm.1), kind=kOutput, calls=%fused_computation.11 | convolution fusion | flops 1610612736 | bytes 4194304 | tf_op jit(solution)/shard_map/dot_general | solution.py:380
  5.6 0.0 copy-done
  5.6 0.0 copy-done.1
  5.6 1.8 %fusion.2 = f32[512,512]{1,0:T(8,128)S(1)} fusion(bf16[3072,512]{1,0:T(8,128)(2,1)S(1)} %copy-done, bf16[3072,512]{1,0:T(8,128)(2,1)S(1)} %copy-done.1), kind=kOutput, calls=%fused_computation.12 | convolution fusion | flops 1610612736 | bytes 7340032 | tf_op jit(solution)/shard_map/dot_general | solution.py:383
  7.5 0.1 fusion
  7.5 0.1 pad_maximum_fusion.cross_in
  7.6 52.9 %normal_equations.1 = (f32[512,512]{1,0:T(8,128)S(1)}, f32[2048,128]{1,0:T(8,128)S(1)}) custom-call(f32[1280,128]{1,0:T(8,128)S(1)} %slice_dynamic-update-slice_fusion.1.gram_in, f32[2048,128]{1,0:T(8,128)S(1)} %pad_maximum_fusion.cross_in), custom_call_target="tpu_custom_call" | custom-call | tf_op jit(solution)/shard_map/normal_equations/pallas_call | solution.py:241
  60.5 8.4 %solve_and_residual.1 = (f32[512,512]{1,0:T(8,128)}, bf16[3072,512]{1,0:T(8,128)(2,1)}) custom-call(f32[512,512]{1,0:T(8,128)S(1)} %get-tuple-element.4.inv_ref, f32[2048,128]{1,0:T(8,128)S(1)} %get-tuple-element.5.b_ref, bf16[3072,512]{1,0:T(8,128)(2,1)S(1)} %copy-done, bf16[3072,512]{1,0:T(8,128)(2,1)} %y_hbm.1), custom_call_target="tpu_custom_call" | custom-call | tf_op jit(solution)/shard_map/solve_and_residual/pallas_call | solution.py:356
  (9 shorter events, 0.1 us)
Async XLA Ops:
  0.6 5.0 %copy-start = (bf16[3072,512]{1,0:T(8,128)(2,1)S(1)}, bf16[3072,512]{1,0:T(8,128)(2,1)}, u32[]{:S(2)}) copy-start(bf16[3072,512]{1,0:T(8,128)(2,1)} %x_hbm.1) | copy-start | bytes 9437188
  0.6 5.0 %copy-start.1 = (bf16[3072,512]{1,0:T(8,128)(2,1)S(1)}, bf16[3072,512]{1,0:T(8,128)(2,1)}, u32[]{:S(2)}) copy-start(bf16[3072,512]{1,0:T(8,128)(2,1)} %y_hbm.1) | copy-start | bytes 9437188

commit v5 on v4

--- a/solution.py
+++ b/solution.py
@@ -152,9 +152,40 @@
     return parts, scratch
 
 
+def invert_gram(nk, gram, panel, side, after):
+    panel[...] = jnp.zeros_like(panel)
+    side[...] = jnp.zeros_like(side)
+
+    def update(i):
+        rows = slice(i * BLK, (i + 1) * BLK)
+        gram[rows, :] -= dot32(side[rows, :], panel[...])
+
+    updates = [functools.partial(update, i) for i in range(nk)]
+
+    def stage(j, diagonal):
+        here = pl.ds(pl.multiple_of(j * BLK, BLK), BLK)
+        following = pl.ds(pl.multiple_of(jnp.minimum(j + 1, nk - 1) * BLK, BLK), BLK)
+        inverse = invert_block(diagonal, updates)
+        panel[...] = dot32(inverse, gram[here, :])
+        panel[:, here] = inverse
+        side[...] = gram[:, here]
+        side[here, :] = jnp.zeros_like(inverse)
+        gram[:, here] = jnp.zeros(side.shape, jnp.float32)
+        gram[here, :] = panel[...]
+        diagonal = gram[following, following] - dot32(
+            side[following, :], panel[:, following]
+        )
+        after(j)
+        return diagonal
+
+    lax.fori_loop(0, nk, stage, gram[0:BLK, 0:BLK])
+    for work in updates:
+        work()
+
+
 def normal_kernel(
     n_grp, n_shard, nk, g_parts, c_parts, gram_in, cross_in,
-    gram, cross_out, gram_out, panel, *scratch,
+    gram, cross_out, gram_out, panel, side, *scratch,
 ):
     a, b, c = phases(n_grp, n_shard)
     barrier = pltpu.get_barrier_semaphore()
@@ -198,23 +229,13 @@
             if i != j:
                 gram[j * BLK : (j + 1) * BLK, i * BLK : (i + 1) * BLK] = block.T
 
-    def stage(j, carry):
-        here = pl.ds(pl.multiple_of(j * BLK, BLK), BLK)
-        inverse = invert_block(gram[here, here])
+    def after(j):
         for t in range(min(nk, 4)):
             @pl.when(j == t)
             def _(t=t):
                 csum.step(t + 3)
 
-        panel[...] = dot32(inverse, gram[here, :])
-        panel[:, here] = inverse
-        side = gram[:, here]
-        gram[:, here] = jnp.zeros_like(side)
-        gram[...] -= dot32(side, panel[...])
-        gram[here, :] = panel[...]
-        return carry
-
-    lax.fori_loop(0, nk, stage, 0)
+    invert_gram(nk, gram, panel, side, after)
     for i in range(nk):
         for j in range(nk):
             gram[i * BLK : (i + 1) * BLK, j * BLK : (j + 1) * BLK] *= down[i] * across[j]
@@ -249,6 +270,7 @@
         scratch_shapes=[
             pltpu.VMEM((padded, BLK), jnp.float32),
             pltpu.VMEM((BLK, k), jnp.float32),
+            pltpu.VMEM((k, BLK), jnp.float32),
             *g_scratch,
             *c_scratch,
         ],
@@ -265,12 +287,15 @@
     return r * (2.0 - p * r)
 
 
-def invert_block(a):
+def invert_block(a, beside=()):
     sub = lax.broadcasted_iota(jnp.int32, (GRP8, BLK), 0)
     lane8 = lax.broadcasted_iota(jnp.int32, (GRP8, BLK), 1)
     lane = lax.broadcasted_iota(jnp.int32, (BLK, BLK), 1)
     for g in range(BLK // GRP8):
         lo = g * GRP8
+        for t, work in enumerate(beside):
+            if t * (BLK // GRP8) // len(beside) == g:
+                work()
         cols = [
             jnp.broadcast_to(a[:, lo + c : lo + c + 1], (BLK, BLK)) for c in range(GRP8)
         ]

time: 70.1 us -> 68.2 us (0.973)
  Pallas kernels: 61.3 us -> 59.4 us
    pallas_call x1, Pallas kernels: 52.9 us -> 51 us  [normal_equations(): pl.pallas_call(functools.partial(normal_kernel, n_grp, n_shard, nk, g_par...]
where the time goes in v5:
time: 68.2 us; the launch traced here: 67.1 us
  Pallas kernels  59.4 us (87%)
  matrix products  6.6 us (10%)
  between operations  0.92 us (1%)
    pallas_call x1, Pallas kernels, normal_equations(): pl.pallas_call(functools.partial(normal_kernel, n_grp, n_shard, nk, g_par...  51 us
    pallas_call x1, Pallas kernels, solve(): pl.pallas_call(functools.partial(solve_kernel, k // BLK, p // BLK, tiles)...  8.38 us
    dot_general x1, matrix products, body(): lax.dot_general(regressors, regressors, contract, preferred_element_type=...  4.8 us
    dot_general x1, matrix products, body(): lax.dot_general(regressors, targets, contract, preferred_element_type=jnp...  1.81 us

profile of v5, /device:TPU:0, one launch (start us, length us, event | category | flops | bytes accessed | tf_op | source)
XLA Modules:
  0.0 67.1 jit_solution(548063440309324706)
XLA Ops:
  0.6 0.0 copy-start
  0.6 0.0 copy-start.1
  0.7 4.8 %fusion.1 = f32[512,512]{1,0:T(8,128)S(1)} fusion(bf16[3072,512]{1,0:T(8,128)(2,1)} %x_hbm.1), kind=kOutput, calls=%fused_computation.11 | convolution fusion | flops 1610612736 | bytes 4194304 | tf_op jit(solution)/shard_map/dot_general | solution.py:405
  5.6 0.0 copy-done
  5.6 0.0 copy-done.1
  5.6 1.8 %fusion.2 = f32[512,512]{1,0:T(8,128)S(1)} fusion(bf16[3072,512]{1,0:T(8,128)(2,1)S(1)} %copy-done, bf16[3072,512]{1,0:T(8,128)(2,1)S(1)} %copy-done.1), kind=kOutput, calls=%fused_computation.12 | convolution fusion | flops 1610612736 | bytes 7340032 | tf_op jit(solution)/shard_map/dot_general | solution.py:408
  7.5 0.1 fusion
  7.5 0.1 pad_maximum_fusion.cross_in
  7.6 51.0 %normal_equations.1 = (f32[512,512]{1,0:T(8,128)S(1)}, f32[2048,128]{1,0:T(8,128)S(1)}) custom-call(f32[1280,128]{1,0:T(8,128)S(1)} %slice_dynamic-update-slice_fusion.1.gram_in, f32[2048,128]{1,0:T(8,128)S(1)} %pad_maximum_fusion.cross_in), custom_call_target="tpu_custom_call" | custom-call | tf_op jit(solution)/shard_map/normal_equations/pallas_call | solution.py:262
  58.6 8.4 %solve_and_residual.1 = (f32[512,512]{1,0:T(8,128)}, bf16[3072,512]{1,0:T(8,128)(2,1)}) custom-call(f32[512,512]{1,0:T(8,128)S(1)} %get-tuple-element.4.inv_ref, f32[2048,128]{1,0:T(8,128)S(1)} %get-tuple-element.5.b_ref, bf16[3072,512]{1,0:T(8,128)(2,1)S(1)} %copy-done, bf16[3072,512]{1,0:T(8,128)(2,1)} %y_hbm.1), custom_call_target="tpu_custom_call" | custom-call | tf_op jit(solution)/shard_map/solve_and_residual/pallas_call | solution.py:381
  (9 shorter events, 0.1 us)
Async XLA Ops:
  0.6 5.0 %copy-start = (bf16[3072,512]{1,0:T(8,128)(2,1)S(1)}, bf16[3072,512]{1,0:T(8,128)(2,1)}, u32[]{:S(2)}) copy-start(bf16[3072,512]{1,0:T(8,128)(2,1)} %x_hbm.1) | copy-start | bytes 9437188
  0.6 5.0 %copy-start.1 = (bf16[3072,512]{1,0:T(8,128)(2,1)S(1)}, bf16[3072,512]{1,0:T(8,128)(2,1)}, u32[]{:S(2)}) copy-start(bf16[3072,512]{1,0:T(8,128)(2,1)} %y_hbm.1) | copy-start | bytes 9437188

commit v6 on v5

--- a/solution.py
+++ b/solution.py
@@ -184,9 +184,14 @@
 
 
 def normal_kernel(
-    n_grp, n_shard, nk, g_parts, c_parts, gram_in, cross_in,
-    gram, cross_out, gram_out, panel, side, *scratch,
+    n_grp, n_shard, nk, g_parts, c_parts, gram_in, x_hbm, y_hbm,
+    gram, cross_out, xv, yv, cross_in, gram_out, panel, side, in_sem, *scratch,
 ):
+    load_x = pltpu.make_async_copy(x_hbm, xv, in_sem.at[0])
+    load_y = pltpu.make_async_copy(y_hbm, yv, in_sem.at[1])
+    load_x.start()
+    load_y.start()
+
     a, b, c = phases(n_grp, n_shard)
     barrier = pltpu.get_barrier_semaphore()
     count = 0
@@ -204,13 +209,37 @@
     csum = Sum(cross_in, cross_out, c_parts, orders[: len(c_parts)], scratch[n_first:])
 
     gsum.step(0)
+    load_x.wait()
+    load_y.wait()
+    frames, k = xv.shape
+    used = yv.shape[1] // BLK * k
+    if used < cross_in.shape[0]:
+        cross_in[used:, :] = jnp.zeros((cross_in.shape[0] - used, BLK), jnp.float32)
+
+    def cross_half(h):
+        span = slice(h * (frames // 2), (h + 1) * (frames // 2))
+        part = lax.dot_general(
+            xv[span, :],
+            yv[span, :],
+            (((0,), (0,)), ((), ())),
+            preferred_element_type=jnp.float32,
+        )
+        for j in range(used // k):
+            piece = part[:, j * BLK : (j + 1) * BLK]
+            if h:
+                piece = cross_in[j * k : (j + 1) * k, :] + piece
+            cross_in[j * k : (j + 1) * k, :] = piece
+
+    gsum.step(1)
+    cross_half(0)
+    gsum.step(2)
+    cross_half(1)
+    gsum.step(3)
     csum.step(0)
-    gsum.step(1)
-    gsum.step(2)
+    gsum.step(4)
+    gsum.step(5)
     csum.step(1)
-    for t in (3, 4, 5, 6):
-        gsum.step(t)
-    csum.step(2)
+    gsum.step(6)
 
     eye = lax.broadcasted_iota(jnp.int32, (BLK, BLK), 0) == lax.broadcasted_iota(
         jnp.int32, (BLK, BLK), 1
@@ -229,6 +258,8 @@
             if i != j:
                 gram[j * BLK : (j + 1) * BLK, i * BLK : (i + 1) * BLK] = block.T
 
+    csum.step(2)
+
     def after(j):
         for t in range(min(nk, 4)):
             @pl.when(j == t)
@@ -245,17 +276,16 @@
     csum.finish()
 
 
-def padded_rows(blocks, unit):
-    extra = -blocks.shape[0] % unit
-    return jnp.pad(blocks, ((0, extra), (0, 0))) if extra else blocks
-
-
-def normal_equations(gram_blocks, cross_blocks, k, n_grp, n_shard):
+def normal_equations(gram_blocks, regressors, targets, n_grp, n_shard):
+    frames, k = regressors.shape
+    p = targets.shape[1]
     nk = k // BLK
     unit = 8 * n_grp * n_shard
-    gram_blocks = padded_rows(gram_blocks, unit)
-    cross_blocks = padded_rows(cross_blocks, unit)
-    padded, cross_rows = gram_blocks.shape[0], cross_blocks.shape[0]
+    extra = -gram_blocks.shape[0] % unit
+    if extra:
+        gram_blocks = jnp.pad(gram_blocks, ((0, extra), (0, 0)))
+    padded = gram_blocks.shape[0]
+    cross_rows = -(-(p // BLK * k) // unit) * unit
     g_parts, g_scratch = sum_scratch(padded, n_grp, n_shard)
     c_parts, c_scratch = sum_scratch(cross_rows, n_grp, n_shard)
     in_vmem = pl.BlockSpec(memory_space=pltpu.VMEM)
@@ -265,12 +295,16 @@
             jax.ShapeDtypeStruct((k, k), jnp.float32),
             jax.ShapeDtypeStruct((cross_rows, BLK), jnp.float32),
         ),
-        in_specs=[in_vmem, in_vmem],
+        in_specs=[in_vmem] + [pl.BlockSpec(memory_space=pl.ANY)] * 2,
         out_specs=(in_vmem, in_vmem),
         scratch_shapes=[
+            pltpu.VMEM((frames, k), jnp.bfloat16),
+            pltpu.VMEM((frames, p), jnp.bfloat16),
+            pltpu.VMEM((cross_rows, BLK), jnp.float32),
             pltpu.VMEM((padded, BLK), jnp.float32),
             pltpu.VMEM((BLK, k), jnp.float32),
             pltpu.VMEM((k, BLK), jnp.float32),
+            pltpu.SemaphoreType.DMA((2,)),
             *g_scratch,
             *c_scratch,
         ],
@@ -278,7 +312,7 @@
             collective_id=0, has_side_effects=True, vmem_limit_bytes=44 * 2**20
         ),
         name="normal_equations",
-    )(gram_blocks, cross_blocks)
+    )(gram_blocks, regressors, targets)
 
 
 def reciprocal(p):
@@ -405,11 +439,7 @@
     gram = lax.dot_general(
         regressors, regressors, contract, preferred_element_type=jnp.float32
     )
-    cross = lax.dot_general(
-        regressors, targets, contract, preferred_element_type=jnp.float32
-    )
-    k = gram.shape[0]
-    nk, nt = k // BLK, cross.shape[1] // BLK
+    nk = gram.shape[0] // BLK
 
     def block(i, j):
         return gram[i * BLK : (i + 1) * BLK, j * BLK : (j + 1) * BLK]
@@ -417,10 +447,9 @@
     gram_blocks = jnp.concatenate(
         [block(i, j) for i in range(nk) for j in range(i + 1)], axis=0
     )
-    cross_blocks = jnp.concatenate(
-        [cross[:, j * BLK : (j + 1) * BLK] for j in range(nt)], axis=0
-    )
-    inverse, total = normal_equations(gram_blocks, cross_blocks, k, n_grp, n_shard)
+    inverse, total = normal_equations(
+        gram_blocks, regressors, targets, n_grp, n_shard
+    )
     return solve(inverse, total, regressors, targets)
 
 

time: 68.2 us -> 69.7 us (1.022); the launches traced: 67.1 us -> 69.6 us
  Pallas kernels: 59.4 us -> 63.9 us
  matrix products: 6.6 us -> 4.79 us
    pallas_call x1, Pallas kernels: 51 us -> 55.5 us  [normal_equations(): pl.pallas_call(functools.partial(normal_kernel, n_grp, n_shard, nk, g_par...]
    dot_general x1 -> x0, matrix products: 1.81 us -> none  [body(): lax.dot_general(regressors, targets, contract, preferred_element_type=jnp...]
where the time goes in v6:
time: 69.7 us; the launch traced here: 69.6 us
  Pallas kernels  63.9 us (92%)
  matrix products  4.79 us (7%)
  between operations  0.74 us (1%)
    pallas_call x1, Pallas kernels, normal_equations(): pl.pallas_call(functools.partial(normal_kernel, n_grp, n_shard, nk, g_par...  55.5 us
    pallas_call x1, Pallas kernels, solve(): pl.pallas_call(functools.partial(solve_kernel, k // BLK, p // BLK, tiles)...  8.38 us
    dot_general x1, matrix products, body(): lax.dot_general(regressors, regressors, contract, preferred_element_type=...  4.79 us

profile of v6, /device:TPU:0, one launch (start us, length us, event | category | flops | bytes accessed | tf_op | source)
XLA Modules:
  0.0 69.6 jit_solution(353955721734837902)
XLA Ops:
  0.6 0.0 copy-start
  0.6 0.0 copy-start.1
  0.7 4.8 %fusion = f32[512,512]{1,0:T(8,128)S(1)} fusion(bf16[3072,512]{1,0:T(8,128)(2,1)} %x_hbm.3), kind=kOutput, calls=%fused_computation.9 | convolution fusion | flops 1610612736 | bytes 4194304 | tf_op jit(solution)/shard_map/dot_general | solution.py:439
  5.6 0.0 copy-done
  5.6 0.0 copy-done.1
  5.6 55.5 %normal_equations.1 = (f32[512,512]{1,0:T(8,128)S(1)}, f32[2048,128]{1,0:T(8,128)S(1)}) custom-call(f32[1280,128]{1,0:T(8,128)S(1)} %slice_dynamic-update-slice_fusion.1.gram_in, bf16[3072,512]{1,0:T(8,128)(2,1)S(1)} %copy-done, bf16[3072,512]{1,0:T(8,128)(2,1)S(1)} %copy-done.1), custom_call_target="tpu_custom_call" | custom-call | tf_op jit(solution)/shard_map/normal_equations/pallas_call | solution.py:292
  61.2 8.4 %solve_and_residual.1 = (f32[512,512]{1,0:T(8,128)}, bf16[3072,512]{1,0:T(8,128)(2,1)}) custom-call(f32[512,512]{1,0:T(8,128)S(1)} %get-tuple-element.4.inv_ref, f32[2048,128]{1,0:T(8,128)S(1)} %get-tuple-element.5.b_ref, bf16[3072,512]{1,0:T(8,128)(2,1)S(1)} %copy-done, bf16[3072,512]{1,0:T(8,128)(2,1)} %y_hbm.3), custom_call_target="tpu_custom_call" | custom-call | tf_op jit(solution)/shard_map/solve_and_residual/pallas_call | solution.py:415
  (9 shorter events, 0.1 us)
Async XLA Ops:
  0.6 5.0 %copy-start = (bf16[3072,512]{1,0:T(8,128)(2,1)S(1)}, bf16[3072,512]{1,0:T(8,128)(2,1)}, u32[]{:S(2)}) copy-start(bf16[3072,512]{1,0:T(8,128)(2,1)} %x_hbm.3) | copy-start | bytes 9437188
  0.6 5.0 %copy-start.1 = (bf16[3072,512]{1,0:T(8,128)(2,1)S(1)}, bf16[3072,512]{1,0:T(8,128)(2,1)}, u32[]{:S(2)}) copy-start(bf16[3072,512]{1,0:T(8,128)(2,1)} %y_hbm.3) | copy-start | bytes 9437188
